TPU v7x, 128 devices: a whole 4x4x4 slice. The times are simulated.
128 devices in a mesh: tile: 16 (over y, x), chan: 8 (over z, core).
Axes of the slice: x: 4, y: 4, z: 4, core: 2. Of those that a mesh axis runs over, the one named last changes fastest.
Arguments:
- latents: bfloat16 [16, 16, 8, 128], P('tile'), may hold values from -6 to 6
- durations: int32 [16], replicated, may hold values from 4 to 8
- assignment: int32 [16], replicated, may hold values from 0 to 15, each once
- entry_weight: bfloat16 [27, 512, 16], P(None, 'chan'), may hold values from -0.3125 to 0.3125
- entry_bias: float32 [512], P('chan'), may hold values from -1 to 1
- first_gain: float32 [512], P('chan'), may hold values from 0.4 to 1.6
- first_shift: float32 [512], P('chan'), may hold values from -0.5 to 0.5
- mixer_weight: bfloat16 [27, 512, 512], P(None, 'chan'), may hold values from -0.0546875 to 0.0546875
- mixer_bias: float32 [512], P('chan'), may hold values from -1 to 1
- second_gain: float32 [512], P('chan'), may hold values from 0.4 to 1.6
- second_shift: float32 [512], P('chan'), may hold values from -0.5 to 0.5
Outputs:
- decoded_frames: bfloat16 [16, 512, 8, 512], P('tile', 'chan')
Inputs may be any that keep to these rules, and one draw needn't show every extreme that they name: `assignment`: each tile number appears exactly once.
All inputs are finite; a program needn't handle non-finite values.
Results may differ from a plain program's by a relative error of at most 0.005.
Values may be sent and summed in bfloat16 or wider, within the bound.
A program may use at most 128 MiB of HBM per device.

v0:
```python
import functools

import jax
import jax.numpy as jnp
from jax import lax
from jax.experimental import pallas as pl
from jax.experimental.pallas import tpu as pltpu
from jax.sharding import PartitionSpec as P

MESH = pl.DeviceIdType.MESH
GSIZE = 16
OV = 3
FT = 8
WT = 16
CELLS = 128
CL = 16
COUT = 64
CIN = 512
KE = 512
WROWS = 432
EPS = 1e-06


def three_parts(x):
    hi = x.astype(jnp.bfloat16).astype(jnp.float32)
    rest = x - hi
    mid = rest.astype(jnp.bfloat16).astype(jnp.float32)
    return hi, mid, rest - mid


def gather_kernel(
    tiles, chans,
    assign, lat, wt, bias, gain, shift,
    we, sel,
    ext, stage,
    s_lat, r_lat, s_z, r_z, s_sib, r_sib, s_sel, r_sel,
):
    me_t = lax.axis_index("tile")
    me_c = lax.axis_index("chan")
    z, core = me_c // 2, me_c % 2

    barrier = pltpu.get_barrier_semaphore()
    for d in range(1, tiles):
        pl.semaphore_signal(barrier, inc=1, device_id=((me_t + d) % tiles, me_c), device_id_type=MESH)
    for d in range(1, chans):
        pl.semaphore_signal(barrier, inc=1, device_id=(me_t, (me_c + d) % chans), device_id_type=MESH)

    ext[:WROWS, :] = wt[...]
    row = lax.broadcasted_iota(jnp.int32, (16, COUT), 0)
    packed = jnp.zeros((16, COUT), jnp.float32)
    for base, ref in ((0, bias), (3, gain), (6, shift)):
        for at, part in enumerate(three_parts(ref[...])):
            packed = jnp.where(row == base + at, part, packed)
    ext[WROWS:WROWS + 16, :] = packed.astype(jnp.bfloat16)
    ext[WROWS + 16:, :] = jnp.zeros((KE - WROWS - 16, COUT), jnp.bfloat16)
    eye = (
        lax.broadcasted_iota(jnp.int32, (COUT, COUT), 0)
        == lax.broadcasted_iota(jnp.int32, (COUT, COUT), 1)
    ).astype(jnp.bfloat16)
    mine = pl.ds(pl.multiple_of(me_c * COUT, COUT), COUT)
    we[mine, :] = lax.dot_general(
        eye, ext[...], (((1,), (1,)), ((), ())), preferred_element_type=jnp.float32
    ).astype(jnp.bfloat16)
    part_rows = CL // chans
    stage[me_t] = lat[pl.ds(me_c * part_rows, part_rows)]

    pl.semaphore_wait(barrier, tiles + chans - 2)

    lat_copies = []
    for d in range(1, tiles):
        copy = pltpu.make_async_remote_copy(
            src_ref=lat.at[pl.ds(me_c * part_rows, part_rows)],
            dst_ref=stage.at[me_t],
            send_sem=s_lat.at[d - 1], recv_sem=r_lat.at[d - 1],
            device_id=((me_t + d) % tiles, me_c), device_id_type=MESH,
        )
        copy.start()
        lat_copies.append(copy)

    zs = chans // 2
    z_copies = []
    for d in (1, zs - 1, 2):
        copy = pltpu.make_async_remote_copy(
            src_ref=we.at[mine], dst_ref=we.at[mine],
            send_sem=s_z.at[d - 1], recv_sem=r_z.at[d - 1],
            device_id=(me_t, ((z + d) % zs) * 2 + core), device_id_type=MESH,
        )
        copy.start()
        z_copies.append((d, copy))
    sib = (me_t, z * 2 + 1 - core)
    sib_copies = []

    def to_sibling(d):
        rows = pl.ds(pl.multiple_of((((z + zs - d) % zs) * 2 + core) * COUT, COUT), COUT)
        copy = pltpu.make_async_remote_copy(
            src_ref=we.at[rows], dst_ref=we.at[rows],
            send_sem=s_sib.at[d], recv_sem=r_sib.at[d],
            device_id=sib, device_id_type=MESH,
        )
        copy.start()
        sib_copies.append(copy)

    to_sibling(0)

    for copy in lat_copies:
        copy.wait_recv()
    own = assign[me_t]
    before = jnp.maximum(own - 1, 0)
    sel[me_c, 0] = stage[own]
    sel[me_c, 1] = stage[before]
    sel_copies = []
    for d in range(1, chans):
        copy = pltpu.make_async_remote_copy(
            src_ref=sel.at[me_c], dst_ref=sel.at[me_c],
            send_sem=s_sel.at[d - 1], recv_sem=r_sel.at[d - 1],
            device_id=(me_t, (me_c + d) % chans), device_id_type=MESH,
        )
        copy.start()
        sel_copies.append(copy)

    for d, copy in z_copies:
        copy.wait_recv()
        to_sibling(d)
    for copy in sel_copies + sib_copies:
        copy.wait_recv()
    for copy in lat_copies + sel_copies + sib_copies + [c for _, c in z_copies]:
        copy.wait_send()


def decode_kernel(
    durations, assign, slot, we, sel, w3, bias, gain, shift,
    out,
    wm, flat, xe, entry, xc, prod, fine, tails, rows, spread, w_sem,
):
    f32, bf16 = jnp.float32, jnp.bfloat16
    w_copies = [
        pltpu.make_async_copy(w3.at[a], wm.at[:, a * CIN:(a + 1) * CIN], w_sem.at[a]) for a in range(3)
    ]
    for copy in w_copies:
        copy.start()

    lane = lax.broadcasted_iota(jnp.int32, (1, CELLS), 1)
    cell_r, cell_q = lane // WT, lane % WT
    diagonal = lax.broadcasted_iota(jnp.int32, (COUT, COUT), 0) == lax.broadcasted_iota(jnp.int32, (COUT, COUT), 1)

    def column(ref):
        return jnp.sum(jnp.where(diagonal, ref[...], 0.0), axis=1, keepdims=True)

    bias_col, gain_col, shift_col = column(bias), column(gain), column(shift)
    own = assign[slot[0]]

    def one_tile(j, tile):
        duration = durations[tile]
        duration_f = duration.astype(f32)
        flat[...] = sel[:, j].astype(f32).reshape(CL * FT, CELLS)
        base = jnp.concatenate([flat[pl.ds(f, CL, stride=FT), :] for f in range(FT)], axis=0)
        for s in range(9):
            b, c = s // 3 - 1, s % 3 - 1
            moved = base
            if s != 4:
                moved = pltpu.roll(base, (-(b * WT + c)) % CELLS, 1)
                inside = (cell_r + b >= 0) & (cell_r + b < CELLS // WT) & (cell_q + c >= 0) & (cell_q + c < WT)
                moved = jnp.where(inside, moved, 0.0)
            moved = moved.astype(bf16)
            for a in range(3):
                for f in range(FT):
                    at = max(f - 2 + a, 0)
                    xe[(9 * a + s) * CL:(9 * a + s + 1) * CL, f * CELLS:(f + 1) * CELLS] = moved[at * CL:(at + 1) * CL]
        last = lax.broadcasted_iota(jnp.int32, (KE - WROWS, FT * CELLS), 0)
        xe[WROWS:, :] = jnp.where(last < 3, 1.0, 0.0).astype(bf16)
        entry[...] = jnp.dot(we[...], xe[...], preferred_element_type=f32)

        frame = lax.broadcasted_iota(jnp.int32, (1, 1, FT * CELLS), 2) // CELLS
        live = (frame < duration).astype(f32)
        members = 1.0 / (GSIZE * CELLS * duration_f)

        def chunk(i, _):
            at = pl.ds(pl.multiple_of(i * COUT, COUT), COUT)
            groups = COUT // GSIZE
            e = entry[at, :].reshape(groups, GSIZE, FT * CELLS)
            mean = jnp.sum(e * live, axis=(1, 2), keepdims=True) * members
            centred = e - mean
            var = jnp.sum(centred * centred * live, axis=(1, 2), keepdims=True) * members
            extra = we[at, KE - CELLS:].astype(f32)
            start = WROWS + 3 - (KE - CELLS)
            g1 = jnp.sum(jnp.where((lane >= start) & (lane < start + 3), extra, 0.0), axis=1, keepdims=True)
            b1 = jnp.sum(jnp.where((lane >= start + 3) & (lane < start + 6), extra, 0.0), axis=1, keepdims=True)
            scale = g1.reshape(groups, GSIZE, 1) * lax.rsqrt(var + EPS)
            half = centred * (0.5 * scale) + 0.5 * b1.reshape(groups, GSIZE, 1)
            coarse = (half * jnp.tanh(half) + half).astype(bf16).reshape(COUT, FT * CELLS)
            for a in range(3):
                to = pl.ds(pl.multiple_of(a * CIN + i * COUT, COUT), COUT)
                skip = 2 - a
                for f in range(skip):
                    xc[to, f * CELLS:(f + 1) * CELLS] = coarse[:, :CELLS]
                xc[to, skip * CELLS:] = coarse[:, :(FT - skip) * CELLS]
            return 0

        lax.fori_loop(0, CIN // COUT, chunk, 0)

        prod[...] = jnp.dot(wm[...], xc[...], preferred_element_type=f32)

        total = jnp.zeros((COUT, CELLS), f32)
        top, bottom = cell_r >= 1, cell_r < CELLS // WT - 1
        left, right = cell_q >= 1, cell_q < WT - 1
        for f in range(FT):
            p = [prod[s * COUT:(s + 1) * COUT, f * CELLS:(f + 1) * CELLS] for s in range(9)]
            p[4] = p[4] + bias_col
            upper, lower = [], []
            for c in range(3):
                upper.append(jnp.where(top, pltpu.roll(p[c], WT, 1), 0.0) + (p[3 + c] + p[6 + c]))
                lower.append((p[c] + p[3 + c]) + jnp.where(bottom, pltpu.roll(p[6 + c], CELLS - WT, 1), 0.0))
            phases = []
            for r in (upper, lower):
                phases.append(jnp.where(left, pltpu.roll(r[0], 1, 1), 0.0) + (r[1] + r[2]))
                phases.append((r[0] + r[1]) + jnp.where(right, pltpu.roll(r[2], CELLS - 1, 1), 0.0))
            for n in range(4):
                fine[f, :, n * CELLS:(n + 1) * CELLS] = phases[n]
            total = total + ((phases[0] + phases[1]) + (phases[2] + phases[3])) * (f < duration).astype(f32)

        members = 1.0 / (GSIZE * 4 * CELLS * duration_f)

        def per_group(x):
            x = jnp.sum(x.reshape(COUT // GSIZE, GSIZE, CELLS), axis=(1, 2), keepdims=True) * members
            return jnp.broadcast_to(x, (COUT // GSIZE, GSIZE, 1)).reshape(COUT, 1)

        mean = per_group(total)
        total = jnp.zeros((COUT, CELLS), f32)
        for f in range(FT):
            sums = jnp.zeros((COUT, CELLS), f32)
            for n in range(4):
                centred = fine[f, :, n * CELLS:(n + 1) * CELLS] - mean
                sums = sums + centred * centred
            total = total + sums * (f < duration).astype(f32)
        scale = 0.5 * gain_col * lax.rsqrt(per_group(total) + EPS)
        offset = 0.5 * shift_col

        def finish(f):
            half = (fine[f] - mean) * scale + offset
            return (half * jnp.tanh(half) + half).astype(bf16)

        return duration, finish

    before = jnp.maximum(own - 1, 0)
    for copy in w_copies:
        copy.wait()
    duration, finish = one_tile(1, before)
    for k in range(OV):
        tails[k] = finish(duration - OV + k)
    duration, finish = one_tile(0, own)
    for f in range(FT):
        result = jnp.where(f < duration, finish(f).astype(f32), 0.0)
        if f < OV:
            w = (f + 1) / (OV + 1)
            blended = result * w + tails[f].astype(f32) * (1.0 - w)
            result = jnp.where(own == 0, result, blended)
        rows[f * COUT:(f + 1) * COUT, :] = result.astype(bf16)

    col = lax.broadcasted_iota(jnp.int32, (1, 4 * CELLS), 1)
    fr, fc = col // (2 * WT), col % (2 * WT)
    source = ((fr % 2) * 2 + fc % 2) * CELLS + (fr // 2) * WT + fc // 2
    permute = (lax.broadcasted_iota(jnp.int32, (4 * CELLS, 4 * CELLS), 0) == source).astype(f32).astype(bf16)
    whole = jnp.dot(rows[...], permute, preferred_element_type=f32)
    for f in range(FT):
        for n in range(4):
            spread[n, pl.ds(f, COUT, stride=FT), :] = whole[f * COUT:(f + 1) * COUT, n * CELLS:(n + 1) * CELLS]
    for n in range(4):
        out[:, :, n * CELLS:(n + 1) * CELLS] = spread[n].astype(bf16).reshape(COUT, FT, CELLS)


def gather(assign, lat, wt, bias, gain, shift, tiles, chans):
    vmem = pl.BlockSpec(memory_space=pltpu.VMEM)
    dma = pltpu.SemaphoreType.DMA
    part = CL // chans
    return pl.pallas_call(
        functools.partial(gather_kernel, tiles, chans),
        out_shape=(
            jax.ShapeDtypeStruct((CIN, KE), jnp.bfloat16),
            jax.ShapeDtypeStruct((chans, 2, part, FT, CELLS), jnp.bfloat16),
        ),
        in_specs=[pl.BlockSpec(memory_space=pltpu.SMEM)] + [vmem] * 5,
        out_specs=(vmem, vmem),
        scratch_shapes=[
            pltpu.VMEM((KE, COUT), jnp.bfloat16),
            pltpu.VMEM((tiles, part, FT, CELLS), jnp.bfloat16),
            dma((tiles - 1,)), dma((tiles - 1,)),
            dma((3,)), dma((3,)),
            dma((4,)), dma((4,)),
            dma((chans - 1,)), dma((chans - 1,)),
        ],
        compiler_params=pltpu.CompilerParams(collective_id=0, has_side_effects=True),
    )(assign, lat, wt, bias, gain, shift)


def decode(durations, assign, slot, we, sel, w3, bias, gain, shift):
    vmem = pl.BlockSpec(memory_space=pltpu.VMEM)
    smem = pl.BlockSpec(memory_space=pltpu.SMEM)
    bf16, f32 = jnp.bfloat16, jnp.float32
    return pl.pallas_call(
        decode_kernel,
        out_shape=jax.ShapeDtypeStruct((COUT, FT, 4 * CELLS), bf16),
        in_specs=[smem, smem, smem, vmem, vmem, pl.BlockSpec(memory_space=pl.ANY), vmem, vmem, vmem],
        out_specs=vmem,
        scratch_shapes=[
            pltpu.VMEM((9 * COUT, 3 * CIN), bf16),
            pltpu.VMEM((CL * FT, CELLS), f32),
            pltpu.VMEM((KE, FT * CELLS), bf16),
            pltpu.VMEM((CIN, FT * CELLS), f32),
            pltpu.VMEM((3 * CIN, FT * CELLS), bf16),
            pltpu.VMEM((9 * COUT, FT * CELLS), f32),
            pltpu.VMEM((FT, COUT, 4 * CELLS), f32),
            pltpu.VMEM((OV, COUT, 4 * CELLS), bf16),
            pltpu.VMEM((FT * COUT, 4 * CELLS), bf16),
            pltpu.VMEM((4, FT * COUT, CELLS), f32),
            pltpu.SemaphoreType.DMA((3,)),
        ],
        compiler_params=pltpu.CompilerParams(vmem_limit_bytes=56 * 1024 * 1024),
    )(durations, assign, slot, we, sel, w3, bias, gain, shift)


def solution(mesh):
    tiles, chans = mesh.shape["tile"], mesh.shape["chan"]

    def local(latents, durations, assignment, entry_weight, entry_bias, first_gain, first_shift,
              mixer_weight, mixer_bias, second_gain, second_shift):
        wt = jnp.transpose(entry_weight, (0, 2, 1)).reshape(WROWS, COUT)
        we, sel = gather(
            assignment, latents[0], wt, entry_bias[None], first_gain[None], first_shift[None], tiles, chans
        )
        slot = lax.axis_index("tile").astype(jnp.int32)[None]
        out = decode(
            durations, assignment, slot, we, sel, mixer_weight.reshape(3, 9 * COUT, CIN),
            mixer_bias[None], second_gain[None], second_shift[None],
        )
        return out[None]

    in_specs = (
        P("tile", None, None, None), P(), P(), P(None, "chan", None), P("chan"), P("chan"), P("chan"),
        P(None, "chan", None), P("chan"), P("chan"), P("chan"),
    )
    return jax.shard_map(
        local, mesh=mesh, in_specs=in_specs, out_specs=P("tile", "chan", None, None), check_vma=False
    )
```

profile of v0, /device:TPU:1, one launch (start us, length us, event | category | flops | bytes accessed | tf_op | source)
XLA Modules:
  0.0 33.5 jit_solution(14720678670183133349)
XLA Ops:
  0.0 18.6 %shard_map.109 = (bf16[512,512]{1,0:T(8,128)(2,1)}, bf16[8,2,2,8,128]{4,3,2,1,0:T(8,128)(2,1)}) custom-call(s32[16]{0:T(128)} %assign.3, bf16[16,8,128]{2,1,0:T(8,128)(2,1)} %bitcast.15, bf16[432,64]{1,0:T(8,128)(2,1)} %bitcast.14, f32[1,64]{1,0:T(1,128)} %bitcast.16, f32[1,64]{1,0:T(1,128)} %bitcast.17, f32[1,64]{1,0:T(1,128)} %bitcast.18), custom_call_target="tpu_custom_call" | custom-call | tf_op jit(solution)/shard_map/pallas_call | solution.py:275
  18.6 14.9 %shard_map.110 = bf16[64,8,512]{2,1,0:T(8,128)(2,1)} custom-call(s32[16]{0:T(128)} %durations.1, s32[16]{0:T(128)} %assign.3, s32[1]{0:T(128)} %bitcast.slot, bf16[512,512]{1,0:T(8,128)(2,1)} %get-tuple-element.7.we, bf16[8,2,2,8,128]{4,3,2,1,0:T(8,128)(2,1)} %get-tuple-element.8.sel, bf16[3,576,512]{2,1,0:T(8,128)(2,1)} %bitcast.13, f32[1,64]{1,0:T(1,128)} %bitcast.19, ...), custom_call_target="tpu_custom_call" | custom-call | tf_op jit(solution)/shard_map/pallas_call | solution.py:299
where the time goes:
time: 33.7 us; the launch traced here: 33.5 us
  Pallas kernels  33.5 us (99%)
    pallas_call x1, Pallas kernels, gather(): pl.pallas_call(functools.partial(gather_kernel, tiles, chans), out_shape=...  18.6 us
    pallas_call x1, Pallas kernels, decode(): pl.pallas_call(decode_kernel, out_shape=jax.ShapeDtypeStruct((COUT, FT, 4...  14.9 us

commit v1 on v0

v1 whole, which is shorter than its diff:
```python
import functools

import jax
import jax.numpy as jnp
from jax import lax
from jax.experimental import pallas as pl
from jax.experimental.pallas import tpu as pltpu
from jax.sharding import PartitionSpec as P

MESH = pl.DeviceIdType.MESH
GSIZE = 16
OV = 3
FT = 8
WT = 16
CELLS = 128
CL = 16
COUT = 64
CIN = 512
KE = 512
WROWS = 432
EARLY = 1
EPS = 1e-06


def three_parts(x):
    hi = x.astype(jnp.bfloat16).astype(jnp.float32)
    rest = x - hi
    mid = rest.astype(jnp.bfloat16).astype(jnp.float32)
    return hi, mid, rest - mid


def gather_kernel(
    tiles, chans, prepare_rest,
    assign, lat, wt, bias, gain, shift,
    we, sel,
    ext, stage,
    s_lat, r_lat, s_z, r_z, s_sib, r_sib, s_sel, r_sel, ready,
):
    me_t = lax.axis_index("tile")
    me_c = lax.axis_index("chan")
    z, core = me_c // 2, me_c % 2
    zs = chans // 2
    sibling = (me_t, z * 2 + 1 - core)

    barrier = pltpu.get_barrier_semaphore()

    @pl.when(core == 0)
    def _():
        for d in range(1, zs):
            pl.semaphore_signal(barrier, inc=1, device_id=(me_t, ((z + d) % zs) * 2), device_id_type=MESH)

    @pl.when(core == 1)
    def _():
        pl.semaphore_signal(barrier, inc=1, device_id=sibling, device_id_type=MESH)
        for d in range(1, tiles):
            pl.semaphore_signal(barrier, inc=1, device_id=((me_t + d) % tiles, me_c), device_id_type=MESH)

    ext[:WROWS, :] = wt[...]
    row = lax.broadcasted_iota(jnp.int32, (16, COUT), 0)
    packed = jnp.zeros((16, COUT), jnp.float32)
    for base, ref in ((0, bias), (3, gain), (6, shift)):
        for at, piece in enumerate(three_parts(ref[...])):
            packed = jnp.where(row == base + at, piece, packed)
    ext[WROWS:WROWS + 16, :] = packed.astype(jnp.bfloat16)
    ext[WROWS + 16:, :] = jnp.zeros((KE - WROWS - 16, COUT), jnp.bfloat16)
    eye = (
        lax.broadcasted_iota(jnp.int32, (COUT, COUT), 0)
        == lax.broadcasted_iota(jnp.int32, (COUT, COUT), 1)
    ).astype(jnp.bfloat16)

    def shard(chip, half):
        return pl.ds(pl.multiple_of((chip * 2 + half) * COUT, COUT), COUT)

    we[shard(z, core), :] = lax.dot_general(
        eye, ext[...], (((1,), (1,)), ((), ())), preferred_element_type=jnp.float32
    ).astype(jnp.bfloat16)

    def lat_copy(d):
        return pltpu.make_async_remote_copy(
            src_ref=lat, dst_ref=stage.at[me_t],
            send_sem=s_lat.at[d - 1], recv_sem=r_lat.at[d - 1],
            device_id=((me_t + d) % tiles, me_c), device_id_type=MESH,
        )

    def z_copy(d, half):
        rows = shard(z, half)
        return pltpu.make_async_remote_copy(
            src_ref=we.at[rows], dst_ref=we.at[rows],
            send_sem=s_z.at[d - 1, half], recv_sem=r_z.at[d - 1, half],
            device_id=(me_t, ((z + d) % zs) * 2), device_id_type=MESH,
        )

    def sib_copy(d, half):
        rows = shard((z + zs - d) % zs, half)
        return pltpu.make_async_remote_copy(
            src_ref=we.at[rows], dst_ref=we.at[rows],
            send_sem=s_sib.at[d, half], recv_sem=r_sib.at[d, half],
            device_id=sibling, device_id_type=MESH,
        )

    sel_copy = pltpu.make_async_remote_copy(
        src_ref=sel, dst_ref=sel, send_sem=s_sel, recv_sem=r_sel, device_id=sibling, device_id_type=MESH,
    )
    order = (1, 2, zs - 1)

    prepare_rest()

    @pl.when(core == 0)
    def _():
        pl.semaphore_wait(barrier, zs)
        pl.semaphore_signal(ready, inc=1, device_id=sibling, device_id_type=MESH)
        for d in order:
            z_copy(d, 0).start()
        sib_copy(0, 0).start()
        sib_copy(0, 1).wait_recv()
        for d in order:
            z_copy(d, 1).start()
        for d in order:
            for half in range(2):
                z_copy(d, half).wait_recv()
                sib_copy(d, half).start()
        sel_copy.wait_recv()
        for d in order:
            for half in range(2):
                z_copy(d, half).wait_send()
                sib_copy(d, half).wait_send()
        sib_copy(0, 0).wait_send()

    @pl.when(core == 1)
    def _():
        def send_weights():
            pl.semaphore_wait(ready, 1)
            sib_copy(0, 1).start()

        def send_latents():
            pl.semaphore_wait(barrier, tiles - 1)
            for d in range(1, tiles):
                lat_copy(d).start()

        @pl.when(z < EARLY)
        def _():
            send_latents()
            send_weights()

        @pl.when(z >= EARLY)
        def _():
            send_weights()
            send_latents()

        stage[me_t] = lat[...]
        for d in range(1, tiles):
            lat_copy(d).wait_recv()
        own = assign[me_t]
        sel[0] = stage[own]
        sel[1] = stage[jnp.maximum(own - 1, 0)]
        sel_copy.start()
        sib_copy(0, 0).wait_recv()
        for d in order:
            for half in range(2):
                sib_copy(d, half).wait_recv()
        for d in range(1, tiles):
            lat_copy(d).wait_send()
        sel_copy.wait_send()
        sib_copy(0, 1).wait_send()


def decode_kernel(
    w_copies, durations, assign, we, sel, bias, gain, shift,
    out, wm, flat, xe, entry, xp, prod, fine, tails, rows, spread, permute,
):
    f32, bf16 = jnp.float32, jnp.bfloat16
    lane = lax.broadcasted_iota(jnp.int32, (1, CELLS), 1)
    cell_r, cell_q = lane // WT, lane % WT
    diagonal = lax.broadcasted_iota(jnp.int32, (COUT, COUT), 0) == lax.broadcasted_iota(jnp.int32, (COUT, COUT), 1)

    def column(ref):
        return jnp.sum(jnp.where(diagonal, ref[...], 0.0), axis=1, keepdims=True)

    bias_col, gain_col, shift_col = column(bias), column(gain), column(shift)
    own = assign[lax.axis_index("tile")]
    duration_of = (durations[own], durations[jnp.maximum(own - 1, 0)])
    groups = COUT // GSIZE

    def frame(f):
        return slice(f * CELLS, (f + 1) * CELLS)

    def add_live(terms, duration):
        total = terms[0]
        for f in range(1, FT):
            total = total + (terms[f] if f < FT // 2 else terms[f] * (f < duration).astype(f32))
        return total

    for j in range(2):
        flat[...] = sel[j].astype(f32).reshape(CL * FT, CELLS)
        base = jnp.concatenate([flat[pl.ds(f, CL, stride=FT), :] for f in range(FT)], axis=0)
        for s in range(9):
            b, c = s // 3 - 1, s % 3 - 1
            moved = base
            if s != 4:
                moved = pltpu.roll(base, (-(b * WT + c)) % CELLS, 1)
                inside = (cell_r + b >= 0) & (cell_r + b < CELLS // WT) & (cell_q + c >= 0) & (cell_q + c < WT)
                moved = jnp.where(inside, moved, 0.0)
            moved = moved.astype(bf16)
            for a in range(3):
                for f in range(FT):
                    at = max(f - 2 + a, 0)
                    xe[j, (9 * a + s) * CL:(9 * a + s + 1) * CL, frame(f)] = moved[at * CL:(at + 1) * CL]
        entry[j] = jnp.dot(we[...], xe[j], preferred_element_type=f32)

    chunks = [slice(i * COUT, (i + 1) * COUT) for i in range(CIN // COUT)]

    def group_sum(x, members):
        return jnp.sum(x.reshape(groups, GSIZE, CELLS), axis=(1, 2), keepdims=True) * members

    def spread_rows(x):
        return jnp.broadcast_to(x, (groups, GSIZE, 1)).reshape(COUT, 1)

    means, scales = {}, {}
    members = [1.0 / (GSIZE * CELLS * d.astype(f32)) for d in duration_of]
    for j in range(2):
        for i, at in enumerate(chunks):
            total = add_live([entry[j, at, frame(f)] for f in range(FT)], duration_of[j])
            means[j, i] = spread_rows(group_sum(total, members[j]))
    for j in range(2):
        for i, at in enumerate(chunks):
            squares = []
            for f in range(FT):
                centred = entry[j, at, frame(f)] - means[j, i]
                squares.append(centred * centred)
            var = group_sum(add_live(squares, duration_of[j]), members[j])
            scales[j, i] = spread_rows(0.5 * lax.rsqrt(var + EPS))
    start = WROWS + 3 - (KE - CELLS)
    for i, at in enumerate(chunks):
        extra = we[at, KE - CELLS:].astype(f32)
        g1 = jnp.sum(jnp.where((lane >= start) & (lane < start + 3), extra, 0.0), axis=1, keepdims=True)
        b1 = jnp.sum(jnp.where((lane >= start + 3) & (lane < start + 6), extra, 0.0), axis=1, keepdims=True)
        for j in range(2):
            scale = scales[j, i] * g1
            offset = 0.5 * b1 - means[j, i] * scale
            for f in range(FT):
                half = entry[j, at, frame(f)] * scale + offset
                coarse = (half * jnp.tanh(half) + half).astype(bf16)
                xp[j, at, frame(f + 2)] = coarse
                if f == 0:
                    xp[j, at, frame(0)] = coarse
                    xp[j, at, frame(1)] = coarse

    for copy in w_copies:
        copy.wait()
    top, bottom = cell_r >= 1, cell_r < CELLS // WT - 1
    left, right = cell_q >= 1, cell_q < WT - 1

    def mix(j):
        delayed = jnp.concatenate([xp[j, :, a * CELLS:(a + FT) * CELLS] for a in range(3)], axis=0)
        prod[j] = jnp.dot(wm[...], delayed, preferred_element_type=f32)

    def upsampled(j):
        sums = []
        for f in range(FT):
            p = [prod[j, s * COUT:(s + 1) * COUT, frame(f)] for s in range(9)]
            p[4] = p[4] + bias_col
            upper, lower = [], []
            for c in range(3):
                upper.append(jnp.where(top, pltpu.roll(p[c], WT, 1), 0.0) + (p[3 + c] + p[6 + c]))
                lower.append((p[c] + p[3 + c]) + jnp.where(bottom, pltpu.roll(p[6 + c], CELLS - WT, 1), 0.0))
            phases = []
            for r in (upper, lower):
                phases.append(jnp.where(left, pltpu.roll(r[0], 1, 1), 0.0) + (r[1] + r[2]))
                phases.append((r[0] + r[1]) + jnp.where(right, pltpu.roll(r[2], CELLS - 1, 1), 0.0))
            for n in range(4):
                fine[j, f, :, frame(n)] = phases[n]
            sums.append((phases[0] + phases[1]) + (phases[2] + phases[3]))
        members = 1.0 / (GSIZE * 4 * CELLS * duration_of[j].astype(f32))
        mean = spread_rows(group_sum(add_live(sums, duration_of[j]), members))
        sums = []
        for f in range(FT):
            total = None
            for n in range(4):
                centred = fine[j, f, :, frame(n)] - mean
                total = centred * centred if total is None else total + centred * centred
            sums.append(total)
        var = group_sum(add_live(sums, duration_of[j]), members)
        scale = gain_col * spread_rows(0.5 * lax.rsqrt(var + EPS))
        offset = 0.5 * shift_col - mean * scale

        def finish(f):
            half = fine[j, f] * scale + offset
            return (half * jnp.tanh(half) + half).astype(bf16)

        return finish

    mix(1)
    finish = upsampled(1)
    for k in range(OV):
        tails[k] = finish(jnp.clip(duration_of[1] - OV + k, 0, FT - 1))
    mix(0)
    finish = upsampled(0)
    for f in range(FT):
        result = finish(f).astype(f32)
        if f >= FT // 2:
            result = jnp.where(f < duration_of[0], result, 0.0)
        if f < OV:
            w = (f + 1) / (OV + 1)
            blended = result * w + tails[f].astype(f32) * (1.0 - w)
            result = jnp.where(own == 0, result, blended)
        rows[f * COUT:(f + 1) * COUT, :] = result.astype(bf16)

    whole = jnp.dot(rows[...], permute[...], preferred_element_type=f32)
    for f in range(FT):
        for n in range(4):
            spread[n, pl.ds(f, COUT, stride=FT), :] = whole[f * COUT:(f + 1) * COUT, frame(n)]
    for n in range(4):
        out[:, :, frame(n)] = spread[n].astype(bf16).reshape(COUT, FT, CELLS)


def prepare(xe, permute):
    last = lax.broadcasted_iota(jnp.int32, (KE - WROWS, FT * CELLS), 0)
    ones = jnp.where(last < 3, 1.0, 0.0).astype(jnp.bfloat16)
    for j in range(2):
        xe[j, WROWS:, :] = ones
    col = lax.broadcasted_iota(jnp.int32, (1, 4 * CELLS), 1)
    fr, fc = col // (2 * WT), col % (2 * WT)
    source = ((fr % 2) * 2 + fc % 2) * CELLS + (fr // 2) * WT + fc // 2
    found = lax.broadcasted_iota(jnp.int32, (4 * CELLS, 4 * CELLS), 0) == source
    permute[...] = found.astype(jnp.float32).astype(jnp.bfloat16)


def fused_kernel(
    tiles, chans,
    durations, assign, lat, wt, bias1, gain1, shift1, w3, bias2, gain2, shift2,
    out,
    we, sel, ext, stage,
    wm, flat, xe, entry, xp, prod, fine, tails, rows, spread, permute,
    s_lat, r_lat, s_z, r_z, s_sib, r_sib, s_sel, r_sel, ready, w_sem,
):
    w_copies = [
        pltpu.make_async_copy(w3.at[a], wm.at[:, a * CIN:(a + 1) * CIN], w_sem.at[a]) for a in range(3)
    ]
    for copy in w_copies:
        copy.start()
    gather_kernel(
        tiles, chans, lambda: prepare(xe, permute), assign, lat, wt, bias1, gain1, shift1, we, sel, ext, stage,
        s_lat, r_lat, s_z, r_z, s_sib, r_sib, s_sel, r_sel, ready,
    )
    decode_kernel(
        w_copies, durations, assign, we, sel, bias2, gain2, shift2,
        out, wm, flat, xe, entry, xp, prod, fine, tails, rows, spread, permute,
    )


def fused(tiles, chans, *args):
    vmem = pl.BlockSpec(memory_space=pltpu.VMEM)
    smem = pl.BlockSpec(memory_space=pltpu.SMEM)
    hbm = pl.BlockSpec(memory_space=pl.ANY)
    dma = pltpu.SemaphoreType.DMA
    bf16, f32 = jnp.bfloat16, jnp.float32
    return pl.pallas_call(
        functools.partial(fused_kernel, tiles, chans),
        out_shape=jax.ShapeDtypeStruct((COUT, FT, 4 * CELLS), bf16),
        in_specs=[smem, smem] + [vmem] * 5 + [hbm] + [vmem] * 3,
        out_specs=vmem,
        scratch_shapes=[
            pltpu.VMEM((CIN, KE), bf16),
            pltpu.VMEM((2, CL, FT, CELLS), bf16),
            pltpu.VMEM((KE, COUT), bf16),
            pltpu.VMEM((tiles, CL, FT, CELLS), bf16),
            pltpu.VMEM((9 * COUT, 3 * CIN), bf16),
            pltpu.VMEM((CL * FT, CELLS), f32),
            pltpu.VMEM((2, KE, FT * CELLS), bf16),
            pltpu.VMEM((2, CIN, FT * CELLS), f32),
            pltpu.VMEM((2, CIN, (FT + 2) * CELLS), bf16),
            pltpu.VMEM((2, 9 * COUT, FT * CELLS), f32),
            pltpu.VMEM((2, FT, COUT, 4 * CELLS), f32),
            pltpu.VMEM((OV, COUT, 4 * CELLS), bf16),
            pltpu.VMEM((FT * COUT, 4 * CELLS), bf16),
            pltpu.VMEM((4, FT * COUT, CELLS), f32),
            pltpu.VMEM((4 * CELLS, 4 * CELLS), bf16),
            dma((tiles - 1,)), dma((tiles - 1,)),
            dma((3, 2)), dma((3, 2)),
            dma((4, 2)), dma((4, 2)),
            dma, dma, pltpu.SemaphoreType.REGULAR,
            dma((3,)),
        ],
        compiler_params=pltpu.CompilerParams(
            collective_id=0, has_side_effects=True, vmem_limit_bytes=56 * 1024 * 1024
        ),
    )(*args)


def solution(mesh):
    tiles, chans = mesh.shape["tile"], mesh.shape["chan"]

    def local(latents, durations, assignment, entry_weight, entry_bias, first_gain, first_shift,
              mixer_weight, mixer_bias, second_gain, second_shift):
        wt = jnp.transpose(entry_weight, (0, 2, 1)).reshape(WROWS, COUT)
        out = fused(
            tiles, chans, durations, assignment, latents[0], wt, entry_bias[None], first_gain[None],
            first_shift[None], mixer_weight.reshape(3, 9 * COUT, CIN), mixer_bias[None], second_gain[None],
            second_shift[None],
        )
        return out[None]

    in_specs = (
        P("tile", None, None, None), P(), P(), P(None, "chan", None), P("chan"), P("chan"), P("chan"),
        P(None, "chan", None), P("chan"), P("chan"), P("chan"),
    )
    return jax.shard_map(
        local, mesh=mesh, in_specs=in_specs, out_specs=P("tile", "chan", None, None), check_vma=False
    )
```

time: 33.7 us -> 24.6 us (0.73)
  Pallas kernels: 33.5 us -> 22.5 us
  local copies, waits for them, and re-layouts: 0 us -> 1.87 us
    pallas_call x2 -> x1, Pallas kernels: 33.5 us -> 22.5 us  [fused(): pl.pallas_call(functools.partial(fused_kernel, tiles, chans), out_shape=j...]
    unnamed x0 -> x1, local copies, waits for them, and re-layouts: none -> 1.87 us
where the time goes in v1:
time: 24.6 us; the launch traced here: 24.4 us
  Pallas kernels  22.5 us (91%)
  local copies, waits for them, and re-layouts  1.87 us (8%)
    pallas_call x1, Pallas kernels, fused(): pl.pallas_call(functools.partial(fused_kernel, tiles, chans), out_shape=j...  22.5 us
    unnamed x1, local copies, waits for them, and re-layouts  1.87 us

profile of v1, /device:TPU:1, one launch (start us, length us, event | category | flops | bytes accessed | tf_op | source)
XLA Modules:
  0.0 24.4 jit_solution(2130849355728267491)
XLA Ops:
  0.0 22.5 %shard_map.109 = bf16[64,8,512]{2,1,0:T(8,128)(2,1)} custom-call(s32[16]{0:T(128)} %durations.1, s32[16]{0:T(128)} %assign.1, bf16[16,8,128]{2,1,0:T(8,128)(2,1)} %bitcast.15, bf16[432,64]{1,0:T(8,128)(2,1)} %bitcast.14, f32[1,64]{1,0:T(1,128)} %bitcast.16, f32[1,64]{1,0:T(1,128)} %bitcast.17, f32[1,64]{1,0:T(1,128)} %bitcast.18, ...), custom_call_target="tpu_custom_call" | custom-call | tf_op jit(solution)/shard_map/pallas_call | solution.py:357
  22.5 1.9 %copy.13 = bf16[1,64,8,512]{3,2,1,0:T(8,128)(2,1)} copy(bf16[1,64,8,512]{3,2,1,0:T(8,128)(2,1)} %bitcast.12) | data formatting | bytes 1048576

commit v2 on v1

--- a/solution.py
+++ b/solution.py
@@ -30,8 +30,8 @@
 
 
 def gather_kernel(
-    tiles, chans, prepare_rest,
-    assign, lat, wt, bias, gain, shift,
+    tiles, chans, prepare_rest, start_loads, loads, own_copy,
+    assign, lat, params,
     we, sel,
     ext, stage,
     s_lat, r_lat, s_z, r_z, s_sib, r_sib, s_sel, r_sel, ready,
@@ -55,12 +55,14 @@
         for d in range(1, tiles):
             pl.semaphore_signal(barrier, inc=1, device_id=((me_t + d) % tiles, me_c), device_id_type=MESH)
 
-    ext[:WROWS, :] = wt[...]
+    start_loads()
+    for copy in loads:
+        copy.wait()
     row = lax.broadcasted_iota(jnp.int32, (16, COUT), 0)
     packed = jnp.zeros((16, COUT), jnp.float32)
-    for base, ref in ((0, bias), (3, gain), (6, shift)):
-        for at, piece in enumerate(three_parts(ref[...])):
-            packed = jnp.where(row == base + at, piece, packed)
+    for n in range(3):
+        for at, piece in enumerate(three_parts(params[n])):
+            packed = jnp.where(row == 3 * n + at, piece, packed)
     ext[WROWS:WROWS + 16, :] = packed.astype(jnp.bfloat16)
     ext[WROWS + 16:, :] = jnp.zeros((KE - WROWS - 16, COUT), jnp.bfloat16)
     eye = (
@@ -128,6 +130,8 @@
 
     @pl.when(core == 1)
     def _():
+        own_copy.start()
+
         def send_weights():
             pl.semaphore_wait(ready, 1)
             sib_copy(0, 1).start()
@@ -147,7 +151,7 @@
             send_weights()
             send_latents()
 
-        stage[me_t] = lat[...]
+        own_copy.wait()
         for d in range(1, tiles):
             lat_copy(d).wait_recv()
         own = assign[me_t]
@@ -165,7 +169,7 @@
 
 
 def decode_kernel(
-    w_copies, durations, assign, we, sel, bias, gain, shift,
+    w_copies, durations, assign, we, sel, params,
     out, wm, flat, xe, entry, xp, prod, fine, tails, rows, spread, permute,
 ):
     f32, bf16 = jnp.float32, jnp.bfloat16
@@ -174,9 +178,9 @@
     diagonal = lax.broadcasted_iota(jnp.int32, (COUT, COUT), 0) == lax.broadcasted_iota(jnp.int32, (COUT, COUT), 1)
 
     def column(ref):
-        return jnp.sum(jnp.where(diagonal, ref[...], 0.0), axis=1, keepdims=True)
-
-    bias_col, gain_col, shift_col = column(bias), column(gain), column(shift)
+        return jnp.sum(jnp.where(diagonal, ref, 0.0), axis=1, keepdims=True)
+
+    bias_col, gain_col, shift_col = (column(params[n]) for n in range(3, 6))
     own = assign[lax.axis_index("tile")]
     duration_of = (durations[own], durations[jnp.maximum(own - 1, 0)])
     groups = COUT // GSIZE
@@ -327,39 +331,51 @@
 
 def fused_kernel(
     tiles, chans,
-    durations, assign, lat, wt, bias1, gain1, shift1, w3, bias2, gain2, shift2,
+    durations_in, assign_in, lat, wt, bias1, gain1, shift1, w3, bias2, gain2, shift2,
     out,
-    we, sel, ext, stage,
+    durations, assign, params, we, sel, ext, stage,
     wm, flat, xe, entry, xp, prod, fine, tails, rows, spread, permute,
-    s_lat, r_lat, s_z, r_z, s_sib, r_sib, s_sel, r_sel, ready, w_sem,
+    s_lat, r_lat, s_z, r_z, s_sib, r_sib, s_sel, r_sel, ready, w_sem, load_sem,
 ):
+    me_t = lax.axis_index("tile")
+    loads = [pltpu.make_async_copy(wt, ext.at[:WROWS], load_sem.at[0])]
+    for n, ref in enumerate((bias1, gain1, shift1, bias2, gain2, shift2)):
+        loads.append(pltpu.make_async_copy(ref, params.at[n], load_sem.at[n + 1]))
+    loads.append(pltpu.make_async_copy(durations_in, durations, load_sem.at[7]))
+    loads.append(pltpu.make_async_copy(assign_in, assign, load_sem.at[8]))
+    own_copy = pltpu.make_async_copy(lat, stage.at[me_t], load_sem.at[9])
     w_copies = [
         pltpu.make_async_copy(w3.at[a], wm.at[:, a * CIN:(a + 1) * CIN], w_sem.at[a]) for a in range(3)
     ]
-    for copy in w_copies:
-        copy.start()
+
+    def start_loads():
+        for copy in loads + w_copies:
+            copy.start()
+
     gather_kernel(
-        tiles, chans, lambda: prepare(xe, permute), assign, lat, wt, bias1, gain1, shift1, we, sel, ext, stage,
+        tiles, chans, lambda: prepare(xe, permute), start_loads, loads, own_copy, assign, lat, params, we, sel, ext, stage,
         s_lat, r_lat, s_z, r_z, s_sib, r_sib, s_sel, r_sel, ready,
     )
     decode_kernel(
-        w_copies, durations, assign, we, sel, bias2, gain2, shift2,
+        w_copies, durations, assign, we, sel, params,
         out, wm, flat, xe, entry, xp, prod, fine, tails, rows, spread, permute,
     )
 
 
 def fused(tiles, chans, *args):
     vmem = pl.BlockSpec(memory_space=pltpu.VMEM)
-    smem = pl.BlockSpec(memory_space=pltpu.SMEM)
     hbm = pl.BlockSpec(memory_space=pl.ANY)
     dma = pltpu.SemaphoreType.DMA
     bf16, f32 = jnp.bfloat16, jnp.float32
     return pl.pallas_call(
         functools.partial(fused_kernel, tiles, chans),
-        out_shape=jax.ShapeDtypeStruct((COUT, FT, 4 * CELLS), bf16),
-        in_specs=[smem, smem] + [vmem] * 5 + [hbm] + [vmem] * 3,
+        out_shape=pltpu.VMEM((COUT, FT, 4 * CELLS), bf16),
+        in_specs=[hbm] * 11,
         out_specs=vmem,
         scratch_shapes=[
+            pltpu.SMEM((tiles,), jnp.int32),
+            pltpu.SMEM((tiles,), jnp.int32),
+            pltpu.VMEM((6, 1, COUT), f32),
             pltpu.VMEM((CIN, KE), bf16),
             pltpu.VMEM((2, CL, FT, CELLS), bf16),
             pltpu.VMEM((KE, COUT), bf16),
@@ -380,6 +396,7 @@
             dma((4, 2)), dma((4, 2)),
             dma, dma, pltpu.SemaphoreType.REGULAR,
             dma((3,)),
+            dma((10,)),
         ],
         compiler_params=pltpu.CompilerParams(
             collective_id=0, has_side_effects=True, vmem_limit_bytes=56 * 1024 * 1024

time: 24.6 us -> 22 us (0.89)
  Pallas kernels: 22.5 us -> 20.9 us
  local copies, waits for them, and re-layouts: 1.87 us -> 0.8 us
    pallas_call x1, Pallas kernels: 22.5 us -> 20.9 us  [fused(): pl.pallas_call(functools.partial(fused_kernel, tiles, chans), out_shape=p...]
    unnamed x1, local copies, waits for them, and re-layouts: 1.87 us -> 0.8 us
where the time goes in v2:
time: 22 us; the launch traced here: 21.7 us
  Pallas kernels  20.9 us (95%)
  local copies, waits for them, and re-layouts  0.8 us (4%)
    pallas_call x1, Pallas kernels, fused(): pl.pallas_call(functools.partial(fused_kernel, tiles, chans), out_shape=p...  20.9 us
    unnamed x1, local copies, waits for them, and re-layouts  0.8 us

profile of v2, /device:TPU:1, one launch (start us, length us, event | category | flops | bytes accessed | tf_op | source)
XLA Modules:
  0.0 21.7 jit_solution(16418361372831347805)
XLA Ops:
  0.0 20.9 %shard_map.109 = bf16[64,8,512]{2,1,0:T(8,128)(2,1)S(1)} custom-call(s32[16]{0:T(128)} %durations_in.1, s32[16]{0:T(128)} %assign_in.1, bf16[16,8,128]{2,1,0:T(8,128)(2,1)} %bitcast.15, bf16[432,64]{1,0:T(8,128)(2,1)} %bitcast.14, f32[1,64]{1,0:T(1,128)} %bitcast.16, f32[1,64]{1,0:T(1,128)} %bitcast.17, f32[1,64]{1,0:T(1,128)} %bitcast.18, ...), custom_call_target="tpu_custom_call" | custom-call | tf_op jit(solution)/shard_map/pallas_call | solution.py:370
  20.9 0.8 %copy.13 = bf16[1,64,8,512]{3,2,1,0:T(8,128)(2,1)} copy(bf16[1,64,8,512]{3,2,1,0:T(8,128)(2,1)S(1)} %bitcast.12) | data formatting | bytes 1048576

commit v3 on v2

--- a/solution.py
+++ b/solution.py
@@ -19,6 +19,7 @@
 KE = 512
 WROWS = 432
 EARLY = 1
+LATE = 2
 EPS = 1e-06
 
 
@@ -51,82 +52,104 @@
 
     @pl.when(core == 1)
     def _():
-        pl.semaphore_signal(barrier, inc=1, device_id=sibling, device_id_type=MESH)
+        for d in range(zs):
+            pl.semaphore_signal(barrier, inc=1, device_id=(me_t, ((z + d) % zs) * 2), device_id_type=MESH)
         for d in range(1, tiles):
             pl.semaphore_signal(barrier, inc=1, device_id=((me_t + d) % tiles, me_c), device_id_type=MESH)
 
     start_loads()
-    for copy in loads:
-        copy.wait()
-    row = lax.broadcasted_iota(jnp.int32, (16, COUT), 0)
-    packed = jnp.zeros((16, COUT), jnp.float32)
-    for n in range(3):
-        for at, piece in enumerate(three_parts(params[n])):
-            packed = jnp.where(row == 3 * n + at, piece, packed)
-    ext[WROWS:WROWS + 16, :] = packed.astype(jnp.bfloat16)
-    ext[WROWS + 16:, :] = jnp.zeros((KE - WROWS - 16, COUT), jnp.bfloat16)
-    eye = (
-        lax.broadcasted_iota(jnp.int32, (COUT, COUT), 0)
-        == lax.broadcasted_iota(jnp.int32, (COUT, COUT), 1)
-    ).astype(jnp.bfloat16)
 
     def shard(chip, half):
         return pl.ds(pl.multiple_of((chip * 2 + half) * COUT, COUT), COUT)
 
-    we[shard(z, core), :] = lax.dot_general(
-        eye, ext[...], (((1,), (1,)), ((), ())), preferred_element_type=jnp.float32
-    ).astype(jnp.bfloat16)
+    def pack_weights():
+        for copy in loads:
+            copy.wait()
+        row = lax.broadcasted_iota(jnp.int32, (16, COUT), 0)
+        packed = jnp.zeros((16, COUT), jnp.float32)
+        for n in range(3):
+            for at, piece in enumerate(three_parts(params[n])):
+                packed = jnp.where(row == 3 * n + at, piece, packed)
+        ext[WROWS:WROWS + 16, :] = packed.astype(jnp.bfloat16)
+        ext[WROWS + 16:, :] = jnp.zeros((KE - WROWS - 16, COUT), jnp.bfloat16)
+        eye = (
+            lax.broadcasted_iota(jnp.int32, (COUT, COUT), 0)
+            == lax.broadcasted_iota(jnp.int32, (COUT, COUT), 1)
+        ).astype(jnp.bfloat16)
+
+        we[shard(z, core), :] = lax.dot_general(
+            eye, ext[...], (((1,), (1,)), ((), ())), preferred_element_type=jnp.float32
+        ).astype(jnp.bfloat16)
+
+    reach = sorted(range(1, tiles), key=lambda d: -(min(d // 4, 4 - d // 4) + min(d % 4, 4 - d % 4)))
+
+    def lat_peer(d):
+        y = (me_t // 4 + d // 4) % 4
+        return y * 4 + (me_t + d) % 4
 
     def lat_copy(d):
         return pltpu.make_async_remote_copy(
             src_ref=lat, dst_ref=stage.at[me_t],
             send_sem=s_lat.at[d - 1], recv_sem=r_lat.at[d - 1],
-            device_id=((me_t + d) % tiles, me_c), device_id_type=MESH,
+            device_id=(lat_peer(d), me_c), device_id_type=MESH,
         )
 
-    def z_copy(d, half):
-        rows = shard(z, half)
+    def z_copy(d):
+        rows = shard(z, core)
         return pltpu.make_async_remote_copy(
             src_ref=we.at[rows], dst_ref=we.at[rows],
-            send_sem=s_z.at[d - 1, half], recv_sem=r_z.at[d - 1, half],
-            device_id=(me_t, ((z + d) % zs) * 2), device_id_type=MESH,
+            send_sem=s_z.at[d - 1], recv_sem=r_z.at[d - 1],
+            device_id=(me_t, ((z + d) % zs) * 2 + core), device_id_type=MESH,
         )
 
-    def sib_copy(d, half):
-        rows = shard((z + zs - d) % zs, half)
+    def sib_copy(d):
+        rows = shard((z + zs - d) % zs, core)
         return pltpu.make_async_remote_copy(
             src_ref=we.at[rows], dst_ref=we.at[rows],
-            send_sem=s_sib.at[d, half], recv_sem=r_sib.at[d, half],
+            send_sem=s_sib.at[d], recv_sem=r_sib.at[d],
             device_id=sibling, device_id_type=MESH,
         )
+
+    def send_own():
+        for d in order:
+            z_copy(d).start()
+        sib_copy(0).start()
+
+    def hand_on():
+        for d in order:
+            z_copy(d).wait_recv()
+            sib_copy(d).start()
+
+    def finish_weights():
+        for d in range(zs):
+            sib_copy(d).wait_recv()
 
     sel_copy = pltpu.make_async_remote_copy(
         src_ref=sel, dst_ref=sel, send_sem=s_sel, recv_sem=r_sel, device_id=sibling, device_id_type=MESH,
     )
-    order = (1, 2, zs - 1)
-
-    prepare_rest()
+    order = (2, 1, zs - 1)
 
     @pl.when(core == 0)
     def _():
-        pl.semaphore_wait(barrier, zs)
-        pl.semaphore_signal(ready, inc=1, device_id=sibling, device_id_type=MESH)
-        for d in order:
-            z_copy(d, 0).start()
-        sib_copy(0, 0).start()
-        sib_copy(0, 1).wait_recv()
-        for d in order:
-            z_copy(d, 1).start()
-        for d in order:
-            for half in range(2):
-                z_copy(d, half).wait_recv()
-                sib_copy(d, half).start()
+        def meet():
+            pl.semaphore_wait(barrier, chans - 1)
+            pl.semaphore_signal(ready, inc=1, device_id=sibling, device_id_type=MESH)
+
+        @pl.when(z < LATE)
+        def _():
+            pack_weights()
+            meet()
+
+        @pl.when(z >= LATE)
+        def _():
+            meet()
+            pack_weights()
+
+        send_own()
+        prepare_rest()
+        hand_on()
+        finish_weights()
         sel_copy.wait_recv()
-        for d in order:
-            for half in range(2):
-                z_copy(d, half).wait_send()
-                sib_copy(d, half).wait_send()
-        sib_copy(0, 0).wait_send()
 
     @pl.when(core == 1)
     def _():
@@ -134,23 +157,28 @@
 
         def send_weights():
             pl.semaphore_wait(ready, 1)
-            sib_copy(0, 1).start()
+            send_own()
 
         def send_latents():
             pl.semaphore_wait(barrier, tiles - 1)
-            for d in range(1, tiles):
+            for d in reach:
                 lat_copy(d).start()
 
-        @pl.when(z < EARLY)
+        first = (z < EARLY) | ((z == EARLY) & (me_t % 4 > 0) & (me_t > 3))
+
+        @pl.when(first)
         def _():
             send_latents()
+            pack_weights()
             send_weights()
 
-        @pl.when(z >= EARLY)
+        @pl.when(jnp.logical_not(first))
         def _():
+            pack_weights()
             send_weights()
             send_latents()
 
+        prepare_rest()
         own_copy.wait()
         for d in range(1, tiles):
             lat_copy(d).wait_recv()
@@ -158,14 +186,22 @@
         sel[0] = stage[own]
         sel[1] = stage[jnp.maximum(own - 1, 0)]
         sel_copy.start()
-        sib_copy(0, 0).wait_recv()
+        hand_on()
+        finish_weights()
+
+    def drain():
         for d in order:
-            for half in range(2):
-                sib_copy(d, half).wait_recv()
-        for d in range(1, tiles):
-            lat_copy(d).wait_send()
-        sel_copy.wait_send()
-        sib_copy(0, 1).wait_send()
+            z_copy(d).wait_send()
+        for d in range(zs):
+            sib_copy(d).wait_send()
+
+        @pl.when(core == 1)
+        def _():
+            for d in range(1, tiles):
+                lat_copy(d).wait_send()
+            sel_copy.wait_send()
+
+    return drain
 
 
 def decode_kernel(
@@ -194,7 +230,7 @@
             total = total + (terms[f] if f < FT // 2 else terms[f] * (f < duration).astype(f32))
         return total
 
-    for j in range(2):
+    def im2col(j):
         flat[...] = sel[j].astype(f32).reshape(CL * FT, CELLS)
         base = jnp.concatenate([flat[pl.ds(f, CL, stride=FT), :] for f in range(FT)], axis=0)
         for s in range(9):
@@ -209,9 +245,15 @@
                 for f in range(FT):
                     at = max(f - 2 + a, 0)
                     xe[j, (9 * a + s) * CL:(9 * a + s + 1) * CL, frame(f)] = moved[at * CL:(at + 1) * CL]
-        entry[j] = jnp.dot(we[...], xe[j], preferred_element_type=f32)
 
     chunks = [slice(i * COUT, (i + 1) * COUT) for i in range(CIN // COUT)]
+    pairs = range(FT // 2)
+
+    def pair(n):
+        return slice(n * 2 * CELLS, (n + 1) * 2 * CELLS)
+
+    def enter(j, n):
+        entry[j, :, pair(n)] = jnp.dot(we[...], xe[j, :, pair(n)], preferred_element_type=f32)
 
     def group_sum(x, members):
         return jnp.sum(x.reshape(groups, GSIZE, CELLS), axis=(1, 2), keepdims=True) * members
@@ -219,29 +261,34 @@
     def spread_rows(x):
         return jnp.broadcast_to(x, (groups, GSIZE, 1)).reshape(COUT, 1)
 
-    means, scales = {}, {}
+    means, scales, coefs = {}, {}, {}
     members = [1.0 / (GSIZE * CELLS * d.astype(f32)) for d in duration_of]
-    for j in range(2):
-        for i, at in enumerate(chunks):
-            total = add_live([entry[j, at, frame(f)] for f in range(FT)], duration_of[j])
-            means[j, i] = spread_rows(group_sum(total, members[j]))
-    for j in range(2):
-        for i, at in enumerate(chunks):
-            squares = []
-            for f in range(FT):
-                centred = entry[j, at, frame(f)] - means[j, i]
-                squares.append(centred * centred)
-            var = group_sum(add_live(squares, duration_of[j]), members[j])
-            scales[j, i] = spread_rows(0.5 * lax.rsqrt(var + EPS))
-    start = WROWS + 3 - (KE - CELLS)
-    for i, at in enumerate(chunks):
-        extra = we[at, KE - CELLS:].astype(f32)
+
+    def mean_of(j, i):
+        total = add_live([entry[j, chunks[i], frame(f)] for f in range(FT)], duration_of[j])
+        means[j, i] = spread_rows(group_sum(total, members[j]))
+
+    def scale_of(j, i):
+        squares = []
+        for f in range(FT):
+            centred = entry[j, chunks[i], frame(f)] - means[j, i]
+            squares.append(centred * centred)
+        var = group_sum(add_live(squares, duration_of[j]), members[j])
+        scales[j, i] = spread_rows(0.5 * lax.rsqrt(var + EPS))
+
+    def coef_of(i):
+        start = WROWS + 3 - (KE - CELLS)
+        extra = we[chunks[i], KE - CELLS:].astype(f32)
         g1 = jnp.sum(jnp.where((lane >= start) & (lane < start + 3), extra, 0.0), axis=1, keepdims=True)
         b1 = jnp.sum(jnp.where((lane >= start + 3) & (lane < start + 6), extra, 0.0), axis=1, keepdims=True)
-        for j in range(2):
+        coefs[i] = g1, b1
+
+    def normalise(j, n):
+        for i, at in enumerate(chunks):
+            g1, b1 = coefs[i]
             scale = scales[j, i] * g1
             offset = 0.5 * b1 - means[j, i] * scale
-            for f in range(FT):
+            for f in (2 * n, 2 * n + 1):
                 half = entry[j, at, frame(f)] * scale + offset
                 coarse = (half * jnp.tanh(half) + half).astype(bf16)
                 xp[j, at, frame(f + 2)] = coarse
@@ -249,18 +296,20 @@
                     xp[j, at, frame(0)] = coarse
                     xp[j, at, frame(1)] = coarse
 
-    for copy in w_copies:
-        copy.wait()
     top, bottom = cell_r >= 1, cell_r < CELLS // WT - 1
     left, right = cell_q >= 1, cell_q < WT - 1
 
-    def mix(j):
-        delayed = jnp.concatenate([xp[j, :, a * CELLS:(a + FT) * CELLS] for a in range(3)], axis=0)
-        prod[j] = jnp.dot(wm[...], delayed, preferred_element_type=f32)
-
-    def upsampled(j):
-        sums = []
-        for f in range(FT):
+    def mix(j, n):
+        first = n * 2 * CELLS
+        delayed = jnp.concatenate(
+            [xp[j, :, first + a * CELLS:first + (a + 2) * CELLS] for a in range(3)], axis=0
+        )
+        prod[j, :, pair(n)] = jnp.dot(wm[...], delayed, preferred_element_type=f32)
+
+    sums = {}
+
+    def upsample(j, n):
+        for f in (2 * n, 2 * n + 1):
             p = [prod[j, s * COUT:(s + 1) * COUT, frame(f)] for s in range(9)]
             p[4] = p[4] + bias_col
             upper, lower = [], []
@@ -271,19 +320,21 @@
             for r in (upper, lower):
                 phases.append(jnp.where(left, pltpu.roll(r[0], 1, 1), 0.0) + (r[1] + r[2]))
                 phases.append((r[0] + r[1]) + jnp.where(right, pltpu.roll(r[2], CELLS - 1, 1), 0.0))
-            for n in range(4):
-                fine[j, f, :, frame(n)] = phases[n]
-            sums.append((phases[0] + phases[1]) + (phases[2] + phases[3]))
+            for m in range(4):
+                fine[j, f, :, frame(m)] = phases[m]
+            sums[j, f] = (phases[0] + phases[1]) + (phases[2] + phases[3])
+
+    def finisher(j):
         members = 1.0 / (GSIZE * 4 * CELLS * duration_of[j].astype(f32))
-        mean = spread_rows(group_sum(add_live(sums, duration_of[j]), members))
-        sums = []
+        mean = spread_rows(group_sum(add_live([sums[j, f] for f in range(FT)], duration_of[j]), members))
+        squares = []
         for f in range(FT):
             total = None
             for n in range(4):
                 centred = fine[j, f, :, frame(n)] - mean
                 total = centred * centred if total is None else total + centred * centred
-            sums.append(total)
-        var = group_sum(add_live(sums, duration_of[j]), members)
+            squares.append(total)
+        var = group_sum(add_live(squares, duration_of[j]), members)
         scale = gain_col * spread_rows(0.5 * lax.rsqrt(var + EPS))
         offset = 0.5 * shift_col - mean * scale
 
@@ -293,12 +344,45 @@
 
         return finish
 
-    mix(1)
-    finish = upsampled(1)
-    for k in range(OV):
-        tails[k] = finish(jnp.clip(duration_of[1] - OV + k, 0, FT - 1))
-    mix(0)
-    finish = upsampled(0)
+    im2col(1)
+    im2col(0)
+    for n in pairs:
+        enter(1, n)
+    for i in range(len(chunks)):
+        mean_of(1, i)
+        coef_of(i)
+        if i % 2:
+            enter(0, i // 2)
+    for i in range(len(chunks)):
+        scale_of(1, i)
+    normalise(1, 0)
+    for copy in w_copies:
+        copy.wait()
+    for n in pairs:
+        mix(1, n)
+        if n + 1 < len(pairs):
+            normalise(1, n + 1)
+        for i in (2 * n, 2 * n + 1):
+            mean_of(0, i)
+        if n > 0:
+            upsample(1, n - 1)
+    for i in range(len(chunks)):
+        scale_of(0, i)
+    normalise(0, 0)
+    for n in pairs:
+        mix(0, n)
+        if n + 1 < len(pairs):
+            normalise(0, n + 1)
+        if n == 0:
+            upsample(1, len(pairs) - 1)
+        if n == 1:
+            finish = finisher(1)
+            for k in range(OV):
+                tails[k] = finish(jnp.clip(duration_of[1] - OV + k, 0, FT - 1))
+        if n > 0:
+            upsample(0, n - 1)
+    upsample(0, len(pairs) - 1)
+    finish = finisher(0)
     for f in range(FT):
         result = finish(f).astype(f32)
         if f >= FT // 2:
@@ -352,7 +436,7 @@
         for copy in loads + w_copies:
             copy.start()
 
-    gather_kernel(
+    drain = gather_kernel(
         tiles, chans, lambda: prepare(xe, permute), start_loads, loads, own_copy, assign, lat, params, we, sel, ext, stage,
         s_lat, r_lat, s_z, r_z, s_sib, r_sib, s_sel, r_sel, ready,
     )
@@ -360,6 +444,7 @@
         w_copies, durations, assign, we, sel, params,
         out, wm, flat, xe, entry, xp, prod, fine, tails, rows, spread, permute,
     )
+    drain()
 
 
 def fused(tiles, chans, *args):
@@ -392,8 +477,8 @@
             pltpu.VMEM((4, FT * COUT, CELLS), f32),
             pltpu.VMEM((4 * CELLS, 4 * CELLS), bf16),
             dma((tiles - 1,)), dma((tiles - 1,)),
-            dma((3, 2)), dma((3, 2)),
-            dma((4, 2)), dma((4, 2)),
+            dma((3,)), dma((3,)),
+            dma((4,)), dma((4,)),
             dma, dma, pltpu.SemaphoreType.REGULAR,
             dma((3,)),
             dma((10,)),

time: 22 us -> 20.5 us (0.932)
  Pallas kernels: 20.9 us -> 19.3 us
    pallas_call x1, Pallas kernels: 20.9 us -> 19.3 us  [fused(): pl.pallas_call(functools.partial(fused_kernel, tiles, chans), out_shape=p...]
where the time goes in v3:
time: 20.5 us; the launch traced here: 20.1 us
  Pallas kernels  19.3 us (94%)
  local copies, waits for them, and re-layouts  0.8 us (4%)
    pallas_call x1, Pallas kernels, fused(): pl.pallas_call(functools.partial(fused_kernel, tiles, chans), out_shape=p...  19.3 us
    unnamed x1, local copies, waits for them, and re-layouts  0.8 us

profile of v3, /device:TPU:1, one launch (start us, length us, event | category | flops | bytes accessed | tf_op | source)
XLA Modules:
  0.0 20.1 jit_solution(121069746681343720)
XLA Ops:
  0.0 19.3 %shard_map.109 = bf16[64,8,512]{2,1,0:T(8,128)(2,1)S(1)} custom-call(s32[16]{0:T(128)} %durations_in.1, s32[16]{0:T(128)} %assign_in.1, bf16[16,8,128]{2,1,0:T(8,128)(2,1)} %bitcast.15, bf16[432,64]{1,0:T(8,128)(2,1)} %bitcast.14, f32[1,64]{1,0:T(1,128)} %bitcast.16, f32[1,64]{1,0:T(1,128)} %bitcast.17, f32[1,64]{1,0:T(1,128)} %bitcast.18, ...), custom_call_target="tpu_custom_call" | custom-call | tf_op jit(solution)/shard_map/pallas_call | solution.py:455
  19.3 0.8 %copy.13 = bf16[1,64,8,512]{3,2,1,0:T(8,128)(2,1)} copy(bf16[1,64,8,512]{3,2,1,0:T(8,128)(2,1)S(1)} %bitcast.12) | data formatting | bytes 1048576

commit v4 on v3

--- a/solution.py
+++ b/solution.py
@@ -18,7 +18,9 @@
 CIN = 512
 KE = 512
 WROWS = 432
-EARLY = 1
+EARLY = 3
+SIDE = 4
+HALF = CL // 2
 LATE = 2
 EPS = 1e-06
 
@@ -31,10 +33,10 @@
 
 
 def gather_kernel(
-    tiles, chans, prepare_rest, start_loads, loads, own_copy,
+    tiles, chans, prepare_rest, start_loads, loads, own_copies,
     assign, lat, params,
     we, sel,
-    ext, stage,
+    ext, near, far_out, far_in,
     s_lat, r_lat, s_z, r_z, s_sib, r_sib, s_sel, r_sel, ready,
 ):
     me_t = lax.axis_index("tile")
@@ -43,6 +45,12 @@
     zs = chans // 2
     sibling = (me_t, z * 2 + 1 - core)
 
+    place = (me_t % SIDE, me_t // SIDE)
+
+    def along(axis, d):
+        x, y = place
+        return y * SIDE + (x + d) % SIDE if axis == 0 else ((y + d) % SIDE) * SIDE + x
+
     barrier = pltpu.get_barrier_semaphore()
 
     @pl.when(core == 0)
@@ -54,8 +62,9 @@
     def _():
         for d in range(zs):
             pl.semaphore_signal(barrier, inc=1, device_id=(me_t, ((z + d) % zs) * 2), device_id_type=MESH)
-        for d in range(1, tiles):
-            pl.semaphore_signal(barrier, inc=1, device_id=((me_t + d) % tiles, me_c), device_id_type=MESH)
+        for axis in range(2):
+            for d in range(1, SIDE):
+                pl.semaphore_signal(barrier, inc=1, device_id=(along(axis, d), me_c), device_id_type=MESH)
 
     start_loads()
 
@@ -81,18 +90,26 @@
             eye, ext[...], (((1,), (1,)), ((), ())), preferred_element_type=jnp.float32
         ).astype(jnp.bfloat16)
 
-    reach = sorted(range(1, tiles), key=lambda d: -(min(d // 4, 4 - d // 4) + min(d % 4, 4 - d % 4)))
-
-    def lat_peer(d):
-        y = (me_t // 4 + d // 4) % 4
-        return y * 4 + (me_t + d) % 4
-
-    def lat_copy(d):
+    def first_copy(h, d):
         return pltpu.make_async_remote_copy(
-            src_ref=lat, dst_ref=stage.at[me_t],
-            send_sem=s_lat.at[d - 1], recv_sem=r_lat.at[d - 1],
-            device_id=(lat_peer(d), me_c), device_id_type=MESH,
+            src_ref=lat.at[pl.ds(h * HALF, HALF)], dst_ref=near[h].at[place[h]],
+            send_sem=s_lat.at[0, h, d - 1], recv_sem=r_lat.at[0, h, d - 1],
+            device_id=(along(h, d), me_c), device_id_type=MESH,
         )
+
+    def second_copy(h, d):
+        return pltpu.make_async_remote_copy(
+            src_ref=far_out.at[h, d - 1], dst_ref=far_in[h].at[place[1 - h]],
+            send_sem=s_lat.at[1, h, d - 1], recv_sem=r_lat.at[1, h, d - 1],
+            device_id=(along(1 - h, d), me_c), device_id_type=MESH,
+        )
+
+    def wanted(slot):
+        own = assign[slot]
+        return own, jnp.maximum(own - 1, 0)
+
+    def spot(axis, tile):
+        return tile % SIDE if axis == 0 else tile // SIDE
 
     def z_copy(d):
         rows = shard(z, core)
@@ -128,6 +145,7 @@
         src_ref=sel, dst_ref=sel, send_sem=s_sel, recv_sem=r_sel, device_id=sibling, device_id_type=MESH,
     )
     order = (2, 1, zs - 1)
+    turns = (2, 1, SIDE - 1)
 
     @pl.when(core == 0)
     def _():
@@ -153,18 +171,20 @@
 
     @pl.when(core == 1)
     def _():
-        own_copy.start()
+        for copy in own_copies:
+            copy.start()
 
         def send_weights():
             pl.semaphore_wait(ready, 1)
             send_own()
 
         def send_latents():
-            pl.semaphore_wait(barrier, tiles - 1)
-            for d in reach:
-                lat_copy(d).start()
-
-        first = (z < EARLY) | ((z == EARLY) & (me_t % 4 > 0) & (me_t > 3))
+            pl.semaphore_wait(barrier, 2 * (SIDE - 1))
+            for d in turns:
+                for h in range(2):
+                    first_copy(h, d).start()
+
+        first = z < EARLY
 
         @pl.when(first)
         def _():
@@ -179,12 +199,22 @@
             send_latents()
 
         prepare_rest()
-        own_copy.wait()
-        for d in range(1, tiles):
-            lat_copy(d).wait_recv()
-        own = assign[me_t]
-        sel[0] = stage[own]
-        sel[1] = stage[jnp.maximum(own - 1, 0)]
+        for copy in own_copies:
+            copy.wait()
+        for h in range(2):
+            for d in turns:
+                first_copy(h, d).wait_recv()
+            for d in turns:
+                for j, tile in enumerate(wanted(along(1 - h, d))):
+                    far_out[h, d - 1, j] = near[h][spot(h, tile)]
+                second_copy(h, d).start()
+            for j, tile in enumerate(wanted(me_t)):
+                far_in[h][place[1 - h], j] = near[h][spot(h, tile)]
+        for h in range(2):
+            for d in turns:
+                second_copy(h, d).wait_recv()
+            for j, tile in enumerate(wanted(me_t)):
+                sel[j, h * HALF:(h + 1) * HALF] = far_in[h][spot(1 - h, tile), j]
         sel_copy.start()
         hand_on()
         finish_weights()
@@ -197,8 +227,10 @@
 
         @pl.when(core == 1)
         def _():
-            for d in range(1, tiles):
-                lat_copy(d).wait_send()
+            for h in range(2):
+                for d in turns:
+                    first_copy(h, d).wait_send()
+                    second_copy(h, d).wait_send()
             sel_copy.wait_send()
 
     return drain
@@ -206,7 +238,7 @@
 
 def decode_kernel(
     w_copies, durations, assign, we, sel, params,
-    out, wm, flat, xe, entry, xp, prod, fine, tails, rows, spread, permute,
+    out, wm, flat, xe, entry, xp, prod, fine, tails, spread, permute,
 ):
     f32, bf16 = jnp.float32, jnp.bfloat16
     lane = lax.broadcasted_iota(jnp.int32, (1, CELLS), 1)
@@ -306,7 +338,7 @@
         )
         prod[j, :, pair(n)] = jnp.dot(wm[...], delayed, preferred_element_type=f32)
 
-    sums = {}
+    sums, squares, pivots = {}, {}, {}
 
     def upsample(j, n):
         for f in (2 * n, 2 * n + 1):
@@ -323,23 +355,27 @@
             for m in range(4):
                 fine[j, f, :, frame(m)] = phases[m]
             sums[j, f] = (phases[0] + phases[1]) + (phases[2] + phases[3])
+        if n == 0:
+            pivots[j] = spread_rows(group_sum(sums[j, 0] + sums[j, 1], 1.0 / (GSIZE * 8 * CELLS)))
+        for f in (2 * n, 2 * n + 1):
+            total = None
+            for m in range(4):
+                apart = fine[j, f, :, frame(m)] - pivots[j]
+                total = apart * apart if total is None else total + apart * apart
+            squares[j, f] = total
 
     def finisher(j):
         members = 1.0 / (GSIZE * 4 * CELLS * duration_of[j].astype(f32))
-        mean = spread_rows(group_sum(add_live([sums[j, f] for f in range(FT)], duration_of[j]), members))
-        squares = []
-        for f in range(FT):
-            total = None
-            for n in range(4):
-                centred = fine[j, f, :, frame(n)] - mean
-                total = centred * centred if total is None else total + centred * centred
-            squares.append(total)
-        var = group_sum(add_live(squares, duration_of[j]), members)
-        scale = gain_col * spread_rows(0.5 * lax.rsqrt(var + EPS))
+        mean = group_sum(add_live([sums[j, f] for f in range(FT)], duration_of[j]), members)
+        about = group_sum(add_live([squares[j, f] for f in range(FT)], duration_of[j]), members)
+        mean = spread_rows(mean)
+        off = mean - pivots[j]
+        var = jnp.maximum(spread_rows(about) - off * off, 0.0)
+        scale = gain_col * (0.5 * lax.rsqrt(var + EPS))
         offset = 0.5 * shift_col - mean * scale
 
-        def finish(f):
-            half = fine[j, f] * scale + offset
+        def finish(f, at=slice(None)):
+            half = fine[j, f, at] * scale[at] + offset[at]
             return (half * jnp.tanh(half) + half).astype(bf16)
 
         return finish
@@ -383,22 +419,22 @@
             upsample(0, n - 1)
     upsample(0, len(pairs) - 1)
     finish = finisher(0)
-    for f in range(FT):
-        result = finish(f).astype(f32)
-        if f >= FT // 2:
-            result = jnp.where(f < duration_of[0], result, 0.0)
-        if f < OV:
-            w = (f + 1) / (OV + 1)
-            blended = result * w + tails[f].astype(f32) * (1.0 - w)
-            result = jnp.where(own == 0, result, blended)
-        rows[f * COUT:(f + 1) * COUT, :] = result.astype(bf16)
-
-    whole = jnp.dot(rows[...], permute[...], preferred_element_type=f32)
-    for f in range(FT):
-        for n in range(4):
-            spread[n, pl.ds(f, COUT, stride=FT), :] = whole[f * COUT:(f + 1) * COUT, frame(n)]
-    for n in range(4):
-        out[:, :, frame(n)] = spread[n].astype(bf16).reshape(COUT, FT, CELLS)
+    part = COUT // 2
+    for at in (slice(0, part), slice(part, COUT)):
+        for f in range(FT):
+            result = finish(f, at).astype(f32)
+            if f >= FT // 2:
+                result = jnp.where(f < duration_of[0], result, 0.0)
+            if f < OV:
+                w = (f + 1) / (OV + 1)
+                blended = result * w + tails[f, at].astype(f32) * (1.0 - w)
+                result = jnp.where(own == 0, result, blended)
+            for n in range(4):
+                spread[n, pl.ds(at.start * FT + f, part, stride=FT), :] = result[:, frame(n)]
+        whole = slice(at.start * FT, at.stop * FT)
+        rows = jnp.concatenate([spread[n, whole, :].astype(bf16) for n in range(4)], axis=1)
+        moved = jnp.dot(rows, permute[...], preferred_element_type=f32)
+        out[at] = moved.astype(bf16).reshape(part, FT, 4 * CELLS)
 
 
 def prepare(xe, permute):
@@ -417,8 +453,8 @@
     tiles, chans,
     durations_in, assign_in, lat, wt, bias1, gain1, shift1, w3, bias2, gain2, shift2,
     out,
-    durations, assign, params, we, sel, ext, stage,
-    wm, flat, xe, entry, xp, prod, fine, tails, rows, spread, permute,
+    durations, assign, params, we, sel, ext, near0, near1, far_out, far_in0, far_in1,
+    wm, flat, xe, entry, xp, prod, fine, tails, spread, permute,
     s_lat, r_lat, s_z, r_z, s_sib, r_sib, s_sel, r_sel, ready, w_sem, load_sem,
 ):
     me_t = lax.axis_index("tile")
@@ -427,7 +463,11 @@
         loads.append(pltpu.make_async_copy(ref, params.at[n], load_sem.at[n + 1]))
     loads.append(pltpu.make_async_copy(durations_in, durations, load_sem.at[7]))
     loads.append(pltpu.make_async_copy(assign_in, assign, load_sem.at[8]))
-    own_copy = pltpu.make_async_copy(lat, stage.at[me_t], load_sem.at[9])
+    near, far_in = (near0, near1), (far_in0, far_in1)
+    own_copies = [
+        pltpu.make_async_copy(lat.at[pl.ds(h * HALF, HALF)], near[h].at[place], load_sem.at[9 + h])
+        for h, place in enumerate((me_t % SIDE, me_t // SIDE))
+    ]
     w_copies = [
         pltpu.make_async_copy(w3.at[a], wm.at[:, a * CIN:(a + 1) * CIN], w_sem.at[a]) for a in range(3)
     ]
@@ -437,12 +477,13 @@
             copy.start()
 
     drain = gather_kernel(
-        tiles, chans, lambda: prepare(xe, permute), start_loads, loads, own_copy, assign, lat, params, we, sel, ext, stage,
+        tiles, chans, lambda: prepare(xe, permute), start_loads, loads, own_copies, assign, lat, params, we, sel, ext,
+        near, far_out, far_in,
         s_lat, r_lat, s_z, r_z, s_sib, r_sib, s_sel, r_sel, ready,
     )
     decode_kernel(
         w_copies, durations, assign, we, sel, params,
-        out, wm, flat, xe, entry, xp, prod, fine, tails, rows, spread, permute,
+        out, wm, flat, xe, entry, xp, prod, fine, tails, spread, permute,
     )
     drain()
 
@@ -464,7 +505,9 @@
             pltpu.VMEM((CIN, KE), bf16),
             pltpu.VMEM((2, CL, FT, CELLS), bf16),
             pltpu.VMEM((KE, COUT), bf16),
-            pltpu.VMEM((tiles, CL, FT, CELLS), bf16),
+            *[pltpu.VMEM((SIDE, HALF, FT, CELLS), bf16)] * 2,
+            pltpu.VMEM((2, SIDE - 1, 2, HALF, FT, CELLS), bf16),
+            *[pltpu.VMEM((SIDE, 2, HALF, FT, CELLS), bf16)] * 2,
             pltpu.VMEM((9 * COUT, 3 * CIN), bf16),
             pltpu.VMEM((CL * FT, CELLS), f32),
             pltpu.VMEM((2, KE, FT * CELLS), bf16),
@@ -473,15 +516,14 @@
             pltpu.VMEM((2, 9 * COUT, FT * CELLS), f32),
             pltpu.VMEM((2, FT, COUT, 4 * CELLS), f32),
             pltpu.VMEM((OV, COUT, 4 * CELLS), bf16),
-            pltpu.VMEM((FT * COUT, 4 * CELLS), bf16),
             pltpu.VMEM((4, FT * COUT, CELLS), f32),
             pltpu.VMEM((4 * CELLS, 4 * CELLS), bf16),
-            dma((tiles - 1,)), dma((tiles - 1,)),
+            dma((2, 2, SIDE - 1)), dma((2, 2, SIDE - 1)),
             dma((3,)), dma((3,)),
             dma((4,)), dma((4,)),
             dma, dma, pltpu.SemaphoreType.REGULAR,
             dma((3,)),
-            dma((10,)),
+            dma((11,)),
         ],
         compiler_params=pltpu.CompilerParams(
             collective_id=0, has_side_effects=True, vmem_limit_bytes=56 * 1024 * 1024

time: 20.5 us -> 20 us (0.976); the launches traced: 20.1 us -> 19.9 us
    pallas_call x1, Pallas kernels: 19.3 us -> 19.1 us  [fused(): pl.pallas_call(functools.partial(fused_kernel, tiles, chans), out_shape=p...]
where the time goes in v4:
time: 20 us; the launch traced here: 19.9 us
  Pallas kernels  19.1 us (96%)
  local copies, waits for them, and re-layouts  0.8 us (4%)
    pallas_call x1, Pallas kernels, fused(): pl.pallas_call(functools.partial(fused_kernel, tiles, chans), out_shape=p...  19.1 us
    unnamed x1, local copies, waits for them, and re-layouts  0.8 us

profile of v4, /device:TPU:1, one launch (start us, length us, event | category | flops | bytes accessed | tf_op | source)
XLA Modules:
  0.0 19.9 jit_solution(3391907752376913626)
XLA Ops:
  0.0 19.1 %shard_map.109 = bf16[64,8,512]{2,1,0:T(8,128)(2,1)S(1)} custom-call(s32[16]{0:T(128)} %durations_in.1, s32[16]{0:T(128)} %assign_in.1, bf16[16,8,128]{2,1,0:T(8,128)(2,1)} %bitcast.15, bf16[432,64]{1,0:T(8,128)(2,1)} %bitcast.14, f32[1,64]{1,0:T(1,128)} %bitcast.16, f32[1,64]{1,0:T(1,128)} %bitcast.17, f32[1,64]{1,0:T(1,128)} %bitcast.18, ...), custom_call_target="tpu_custom_call" | custom-call | tf_op jit(solution)/shard_map/pallas_call | solution.py:496
  19.1 0.8 %copy.13 = bf16[1,64,8,512]{3,2,1,0:T(8,128)(2,1)} copy(bf16[1,64,8,512]{3,2,1,0:T(8,128)(2,1)S(1)} %bitcast.12) | data formatting | bytes 1048576

commit v5 on v4

--- a/solution.py
+++ b/solution.py
@@ -127,13 +127,17 @@
             device_id=sibling, device_id_type=MESH,
         )
 
+    def other(i):
+        return i + (i >= z).astype(jnp.int32)
+
     def send_own():
-        for d in order:
-            z_copy(d).start()
+        for i in range(zs - 1):
+            z_copy((other(i) - z + zs) % zs).start()
         sib_copy(0).start()
 
     def hand_on():
-        for d in order:
+        for i in range(zs - 1):
+            d = (z - other(i) + zs) % zs
             z_copy(d).wait_recv()
             sib_copy(d).start()
 

time: 20 us -> 19.4 us (0.970)
  Pallas kernels: 19.1 us -> 18.5 us
    pallas_call x1, Pallas kernels: 19.1 us -> 18.5 us  [fused(): pl.pallas_call(functools.partial(fused_kernel, tiles, chans), out_shape=p...]
where the time goes in v5:
time: 19.4 us; the launch traced here: 19.3 us
  Pallas kernels  18.5 us (95%)
  local copies, waits for them, and re-layouts  0.8 us (4%)
    pallas_call x1, Pallas kernels, fused(): pl.pallas_call(functools.partial(fused_kernel, tiles, chans), out_shape=p...  18.5 us
    unnamed x1, local copies, waits for them, and re-layouts  0.8 us

profile of v5, /device:TPU:1, one launch (start us, length us, event | category | flops | bytes accessed | tf_op | source)
XLA Modules:
  0.0 19.3 jit_solution(2533884821635828706)
XLA Ops:
  0.0 18.5 %shard_map.109 = bf16[64,8,512]{2,1,0:T(8,128)(2,1)S(1)} custom-call(s32[16]{0:T(128)} %durations_in.1, s32[16]{0:T(128)} %assign_in.1, bf16[16,8,128]{2,1,0:T(8,128)(2,1)} %bitcast.15, bf16[432,64]{1,0:T(8,128)(2,1)} %bitcast.14, f32[1,64]{1,0:T(1,128)} %bitcast.16, f32[1,64]{1,0:T(1,128)} %bitcast.17, f32[1,64]{1,0:T(1,128)} %bitcast.18, ...), custom_call_target="tpu_custom_call" | custom-call | tf_op jit(solution)/shard_map/pallas_call | solution.py:500
  18.5 0.8 %copy.13 = bf16[1,64,8,512]{3,2,1,0:T(8,128)(2,1)} copy(bf16[1,64,8,512]{3,2,1,0:T(8,128)(2,1)S(1)} %bitcast.12) | data formatting | bytes 1048576

commit v6 on v5

--- a/solution.py
+++ b/solution.py
@@ -21,7 +21,7 @@
 EARLY = 3
 SIDE = 4
 HALF = CL // 2
-LATE = 2
+LATE = 0
 EPS = 1e-06
 
 
@@ -192,8 +192,8 @@
 
         @pl.when(first)
         def _():
+            pack_weights()
             send_latents()
-            pack_weights()
             send_weights()
 
         @pl.when(jnp.logical_not(first))

time: 19.4 us -> 19.6 us (1.010)
  Pallas kernels: 18.5 us -> 18.7 us
where the time goes in v6:
time: 19.6 us; the launch traced here: 19.5 us
  Pallas kernels  18.7 us (95%)
  local copies, waits for them, and re-layouts  0.8 us (4%)
    pallas_call x1, Pallas kernels, fused(): pl.pallas_call(functools.partial(fused_kernel, tiles, chans), out_shape=p...  18.7 us
    unnamed x1, local copies, waits for them, and re-layouts  0.8 us

profile of v6, /device:TPU:1, one launch (start us, length us, event | category | flops | bytes accessed | tf_op | source)
XLA Modules:
  0.0 19.5 jit_solution(8554863884081360126)
XLA Ops:
  0.0 18.7 %shard_map.109 = bf16[64,8,512]{2,1,0:T(8,128)(2,1)S(1)} custom-call(s32[16]{0:T(128)} %durations_in.1, s32[16]{0:T(128)} %assign_in.1, bf16[16,8,128]{2,1,0:T(8,128)(2,1)} %bitcast.15, bf16[432,64]{1,0:T(8,128)(2,1)} %bitcast.14, f32[1,64]{1,0:T(1,128)} %bitcast.16, f32[1,64]{1,0:T(1,128)} %bitcast.17, f32[1,64]{1,0:T(1,128)} %bitcast.18, ...), custom_call_target="tpu_custom_call" | custom-call | tf_op jit(solution)/shard_map/pallas_call | solution.py:500
  18.7 0.8 %copy.13 = bf16[1,64,8,512]{3,2,1,0:T(8,128)(2,1)} copy(bf16[1,64,8,512]{3,2,1,0:T(8,128)(2,1)S(1)} %bitcast.12) | data formatting | bytes 1048576
